TPU v7x, 512 devices: a whole 4x4x16 slice. The times are simulated.
512 devices in a mesh: pm: 2 (over y_lo), ka: 128 (over x, z, core), isdf: 2 (over y_hi).
Axes of the slice: x: 4, y: 4 (y_hi: 2, y_lo: 2; y = y_hi * 2 + y_lo), z: 16, core: 2. Of those that a mesh axis runs over, the one named last changes fastest.
Arguments:
- amplitudes: bfloat16 [2, 2, 2, 256, 64, 256], P('pm', None, None, 'ka'), may hold values from -6 to 6
- conduction: bfloat16 [2, 256, 256, 512], P(None, 'ka', None, 'isdf'), may hold values from -0.375 to 0.375
- valence: bfloat16 [2, 256, 64, 512], P(None, 'ka'), may hold values from -0.75 to 0.75
- energy: float32 [256, 64, 256], P('ka', None, 'isdf'), may hold values from 0.5 to 2.5
- screened: bfloat16 [4, 2, 512, 512], P(None, None, 'isdf'), may hold values from -0.59765625 to 0.59765625
- coulomb: float32 [512, 512], P(None, 'isdf'), may hold values from -0.03125 to 0.03125
- mirror: int32 [256], P('ka'), may hold values from 0 to 255, as said below
- transfer_class: int32 [256, 256], P('ka'), may hold values from 0 to 3, as said below
Outputs:
- response: bfloat16 [2, 2, 2, 256, 64, 256], P('pm', None, None, 'ka', None, 'isdf')
Inputs may be any that keep to these rules, and one draw needn't show every extreme that they name: mirror[mirror[k]] = k; a k-point of block j (the aligned block of 2 k-points that holds it) has its mirror in block 127 - j. transfer_class[k, k2] depends only on (k - k2) mod 256.
All inputs are finite; a program needn't handle non-finite values.
Results may differ from a plain program's by a relative error of at most 0.015.
Values may be sent and summed in bfloat16 or wider, within the bound.
A program may use at most 128 MiB of HBM per device.

v0:
```python
import jax
import jax.numpy as jnp
from jax import lax
from jax.sharding import PartitionSpec as P

REACH = 2
HIGHEST = lax.Precision.HIGHEST


def swapped(block, axis, apart):
    count = lax.axis_size(axis)
    route = []
    for low in range(count):
        high = low | 1 << apart
        if high != low and high < count:
            route += [(low, high), (high, low)]
    return lax.ppermute(block, axis, route)


def shifted(value, axis, by):
    size = lax.axis_size(axis)
    return lax.ppermute(value, axis, [(i, (i + by) % size) for i in range(size)])


def pair_einsum(pattern, left, right, conjugate):

    def single(first, second):
        return jnp.einsum(pattern, first, second, preferred_element_type=jnp.float32)

    if conjugate:
        real_part = single(left[0], right[0]) + single(left[1], right[1])
        imag_part = single(left[1], right[0]) - single(left[0], right[1])
    else:
        real_part = single(left[0], right[0]) - single(left[1], right[1])
        imag_part = single(left[0], right[1]) + single(left[1], right[0])
    return (real_part, imag_part)


def conjugated(field):
    return jnp.stack([field[:, 0], -field[:, 1]], axis=1)


def coefficients(vector, conduction):
    real_part, imag_part = pair_einsum(
        "bkvc,kcm->bkvm", (vector[:, 0], vector[:, 1]), (conduction[0], conduction[1]), False
    )
    return jnp.stack([real_part, imag_part], axis=1).astype(jnp.bfloat16)


def amp_bits(field):
    for bit_number in range(lax.axis_size("ka").bit_length() - 1):
        field = swapped(field, "ka", bit_number)
    return field


def result_bits(field):
    for bit_number in range(lax.axis_size("ka").bit_length() - 1):
        field = swapped(field, "ka", bit_number)
    return field


def per_device(amplitudes, conduction, valence, energy, screened, coulomb, mirror, transfer_class):
    pm_index = lax.axis_index("pm")
    ka_index = lax.axis_index("ka")
    isdf_index = lax.axis_index("isdf")
    ka_count = lax.axis_size("ka")
    kpoint_count = conduction.shape[1]
    mu_count = conduction.shape[3]
    point_count = valence.shape[3]
    cond_share = energy.shape[2]
    vector_count = amplitudes.shape[1]
    is_plus = pm_index == 0
    parity = jnp.where(is_plus, 1.0, -1.0).astype(jnp.float32)
    exchange_weight = jnp.where(is_plus, 4.0, 0.0).astype(jnp.float32)
    local_amps = amplitudes[0]
    partner_amps = swapped(local_amps, "pm", 0)
    partner_side = jnp.where(is_plus, partner_amps, local_amps)
    distant_side = amp_bits(partner_side)
    direct = jnp.where(is_plus, local_amps, partner_amps).astype(jnp.float32)
    local_mirror = mirror - (ka_count - 1 - ka_index) * kpoint_count
    flipped = conjugated(jnp.take(distant_side, local_mirror, axis=2).astype(jnp.float32))
    vector = (direct + parity * flipped).astype(jnp.bfloat16)
    own_coef = coefficients(vector, conduction)
    valence_part = lax.dynamic_slice_in_dim(valence, isdf_index * mu_count, mu_count, 3)
    rho_real = jnp.einsum(
        "kvm,bkvm->bm", valence_part[0], own_coef[:, 0], preferred_element_type=jnp.float32
    )
    rho_real = rho_real + jnp.einsum(
        "kvm,bkvm->bm", valence_part[1], own_coef[:, 1], preferred_element_type=jnp.float32
    )
    rho_imag = jnp.einsum(
        "kvm,bkvm->bm", valence_part[0], own_coef[:, 1], preferred_element_type=jnp.float32
    )
    rho_imag = rho_imag - jnp.einsum(
        "kvm,bkvm->bm", valence_part[1], own_coef[:, 0], preferred_element_type=jnp.float32
    )
    density = jnp.stack([rho_real, rho_imag], axis=1)
    spread = jnp.einsum("nm,brm->brn", coulomb, density, precision=HIGHEST)
    spread = lax.psum(spread, ("ka", "isdf"))
    potential = lax.dynamic_slice_in_dim(spread, isdf_index * mu_count, mu_count, 2)
    class_ids = jnp.arange(screened.shape[0], dtype=jnp.int32)

    def accumulate(totals, coef_block, valence_block, source):
        pair_real, pair_imag = pair_einsum(
            "bqvm,qvn->bqmn",
            (coef_block[:, 0], coef_block[:, 1]),
            (valence_block[0], valence_block[1]),
            True,
        )
        pair_real = pair_real.astype(jnp.bfloat16)
        pair_imag = pair_imag.astype(jnp.bfloat16)
        classes = lax.dynamic_slice_in_dim(transfer_class, source * kpoint_count, kpoint_count, 1)
        selector = (classes[:, :, None] == class_ids).astype(jnp.bfloat16)
        total_real, total_imag = totals
        for visitor in range(kpoint_count):
            chosen = jnp.einsum(
                "kw,wrmn->rkmn", selector[:, visitor], screened, preferred_element_type=jnp.float32
            ).astype(jnp.bfloat16)
            screen_real = chosen[0][None].astype(jnp.float32)
            screen_imag = chosen[1][None].astype(jnp.float32)
            visit_real = pair_real[:, visitor][:, None].astype(jnp.float32)
            visit_imag = pair_imag[:, visitor][:, None].astype(jnp.float32)
            total_real = total_real + (screen_real * visit_real - screen_imag * visit_imag)
            total_imag = total_imag + (screen_real * visit_imag + screen_imag * visit_real)
        return (total_real, total_imag)

    payload = (vector, conduction, valence)

    def advance(moving, offset):
        return shifted((moving[0], moving[1], moving[2]), "ka", offset)

    def unpack(moving):
        return (coefficients(moving[0], moving[1]), moving[2])

    def visit(totals, moving, distance):
        coef_block, valence_block = unpack(moving)
        source = jnp.mod(ka_index + distance, ka_count)
        return accumulate(totals, coef_block, valence_block, source)

    zero_field = jnp.zeros((vector_count, kpoint_count, mu_count, point_count), jnp.float32)
    totals = accumulate((zero_field, zero_field), own_coef, valence, ka_index)
    below_item = payload
    for count_done in range(REACH):
        below_item = advance(below_item, 1)
        totals = visit(totals, below_item, -(count_done + 1))
    above_item = payload
    for count_done in range(REACH):
        above_item = advance(above_item, -1)
        totals = visit(totals, above_item, count_done + 1)
    sum_real = totals[0].astype(jnp.bfloat16)
    sum_imag = totals[1].astype(jnp.bfloat16)
    back_real, back_imag = pair_einsum(
        "bkmn,kvn->bkvm", (sum_real, sum_imag), (valence[0], valence[1]), False
    )
    potential_real = potential[:, 0][:, None, None, :]
    potential_imag = potential[:, 1][:, None, None, :]
    exchange_real = potential_real * valence_part[0] - potential_imag * valence_part[1]
    exchange_imag = potential_real * valence_part[1] + potential_imag * valence_part[0]
    field_real = (exchange_weight * exchange_real - back_real).astype(jnp.bfloat16)
    field_imag = (exchange_weight * exchange_imag - back_imag).astype(jnp.bfloat16)
    out_real, out_imag = pair_einsum(
        "bkvm,kcm->bkvc", (field_real, field_imag), (conduction[0], conduction[1]), True
    )
    partial_out = jnp.stack([out_real, out_imag], axis=1)
    summed = lax.psum_scatter(
        partial_out.astype(jnp.bfloat16), "isdf", scatter_dimension=4, tiled=True
    ).astype(jnp.float32)
    vector_part = lax.dynamic_slice_in_dim(vector, isdf_index * cond_share, cond_share, 4).astype(
        jnp.float32
    )
    channel_out = (energy[None, None] * vector_part + summed).astype(jnp.bfloat16)
    partner_out = swapped(channel_out, "pm", 0)
    blended = (
        0.5 * (partner_out.astype(jnp.float32) + parity * channel_out.astype(jnp.float32))
    ).astype(jnp.bfloat16)
    distant_out = result_bits(blended)
    reflected = conjugated(jnp.take(distant_out, local_mirror, axis=2))
    result = jnp.where(is_plus, blended, reflected)
    return result[None]


def solution(mesh):
    return jax.shard_map(
        per_device,
        mesh=mesh,
        in_specs=(
            P("pm", None, None, "ka", None, None),
            P(None, "ka", None, "isdf"),
            P(None, "ka", None, None),
            P("ka", None, "isdf"),
            P(None, None, "isdf", None),
            P(None, "isdf"),
            P("ka"),
            P("ka", None),
        ),
        out_specs=P("pm", None, None, "ka", None, "isdf"),
        check_vma=False,
    )
```

profile of v0, /device:TPU:2, one launch (start us, length us, event | category | flops | bytes accessed | tf_op | source)
XLA Modules:
  0.0 1090.2 jit_solution(7875653439164302398)
XLA Ops:
  8.6 10.8 collective-permute-start.15
  21.3 5.8 collective-permute-start.16
  28.1 3.5 collective-permute-start
  32.8 3.2 copy.91
  59.0 3.0 fusion.79
  76.7 6.6 collective-permute-done.2
  87.2 12.3 %collective-permute-done.3 = bf16[2,2,2,64,256]{4,3,0,2,1:T(8,128)(2,1)S(1)} collective-permute-done((bf16[2,2,2,64,256]{4,3,0,2,1:T(8,128)(2,1)S(1)}, bf16[2,2,2,64,256]{4,3,0,2,1:T(8,128)(2,1)S(1)}, u32[]{:S(2)}, u32[]{:S(2)}) %collective-permute-start.3) | collective-permute-done | bytes 262176 | tf_op jit(solution)/shard_map/ppermute | solution.py:17
  104.0 22.7 %collective-permute-done.4 = bf16[2,2,2,64,256]{4,3,0,2,1:T(8,128)(2,1)S(1)} collective-permute-done((bf16[2,2,2,64,256]{4,3,0,2,1:T(8,128)(2,1)S(1)}, bf16[2,2,2,64,256]{4,3,0,2,1:T(8,128)(2,1)S(1)}, u32[]{:S(2)}, u32[]{:S(2)}) %collective-permute-start.4) | collective-permute-done | bytes 262176 | tf_op jit(solution)/shard_map/ppermute | solution.py:17
  126.6 14.7 %collective-permute-start.5 = (bf16[2,2,2,64,256]{4,3,0,2,1:T(8,128)(2,1)S(1)}, bf16[2,2,2,64,256]{4,3,0,2,1:T(8,128)(2,1)S(1)}, u32[]{:S(2)}, u32[]{:S(2)}) collective-permute-start(bf16[2,2,2,64,256]{4,3,0,2,1:T(8,128)(2,1)S(1)} %collective-permute-done.4), channel_id=1, source_target_pairs={{0,32},{32,0},{2,34},{34,2},{4,36},{36,4},{6,38},{38,6},{8,40},{40... | collective-permute-start | bytes 786440 | tf_op jit(solution)/shard_map/ppermute | solution.py:17
  143.4 14.8 %collective-permute-done.5 = bf16[2,2,2,64,256]{4,3,0,2,1:T(8,128)(2,1)S(1)} collective-permute-done((bf16[2,2,2,64,256]{4,3,0,2,1:T(8,128)(2,1)S(1)}, bf16[2,2,2,64,256]{4,3,0,2,1:T(8,128)(2,1)S(1)}, u32[]{:S(2)}, u32[]{:S(2)}) %collective-permute-start.5) | collective-permute-done | bytes 262176 | tf_op jit(solution)/shard_map/ppermute | solution.py:17
  158.2 2.7 collective-permute-start.6
  163.1 5.4 collective-permute-done.6
  168.4 4.2 collective-permute-start.7
  198.8 5.8 collective-permute-start.19
  206.5 5.8 collective-permute-start.18
  228.5 583.0 %psum.7 = f32[2,2,512]{2,1,0:T(2,128)S(1)} all-reduce(f32[2,2,512]{2,1,0:T(2,128)S(1)} %fusion.90), channel_id=1, replica_groups=mesh['pm'=2,'ka'=128,'isdf'=2] {'ka','isdf'}, use_global_device_ids=true, to_apply=%region_0.1 | all-reduce | flops 2048 | bytes 16384 | tf_op jit(solution)/shard_map/psum | solution.py:99
  845.6 5.3 collective-permute-start.17
  878.6 9.2 add_convert_fusion
  887.9 9.5 add_convert_fusion.1
  901.8 92.5 %reduce-scatter.4.cloned.1.call-done = bf16[128,512]{1,0:T(8,128)(2,1)} async-done(((bf16[256,512]{1,0:T(8,128)(2,1)}), bf16[128,512]{1,0:T(8,128)(2,1)}) %reduce-scatter.4.cloned.1.call-update) | async-done | bytes 131088
  999.0 4.7 collective-permute-done.20
  1007.0 3.5 collective-permute-start.22
  1010.4 4.0 collective-permute-done.22
  1014.4 4.4 collective-permute-start.23
  1018.9 5.9 collective-permute-done.23
  1024.7 7.6 collective-permute-start.24
  1032.4 9.9 collective-permute-done.24
  1042.2 12.0 %collective-permute-start.25 = (bf16[2,2,2,64,128]{4,3,0,2,1:T(8,128)(2,1)S(1)}, bf16[2,2,2,64,128]{4,3,0,2,1:T(8,128)(2,1)S(1)}, u32[]{:S(2)}, u32[]{:S(2)}) collective-permute-start(bf16[2,2,2,64,128]{4,3,0,2,1:T(8,128)(2,1)S(1)} %collective-permute-done.24), channel_id=1, source_target_pairs={{0,32},{32,0},{2,34},{34,2},{4,36},{36,4},{6,38},{38,6},{8,40},{40... | collective-permute-start | bytes 393224 | tf_op jit(solution)/shard_map/ppermute | solution.py:17
  1054.2 12.1 %collective-permute-done.25 = bf16[2,2,2,64,128]{4,3,0,2,1:T(8,128)(2,1)S(1)} collective-permute-done((bf16[2,2,2,64,128]{4,3,0,2,1:T(8,128)(2,1)S(1)}, bf16[2,2,2,64,128]{4,3,0,2,1:T(8,128)(2,1)S(1)}, u32[]{:S(2)}, u32[]{:S(2)}) %collective-permute-start.25) | collective-permute-done | bytes 131104 | tf_op jit(solution)/shard_map/ppermute | solution.py:17
  1068.8 4.4 collective-permute-done.26
  1073.2 3.9 collective-permute-start.27
  1077.1 4.4 collective-permute-done.27
  (285 shorter events, 177.7 us)
Async XLA Ops:
  6.5 221.4 %copy-start = (f32[512,256]{1,0:T(8,128)S(1)}, f32[512,256]{1,0:T(8,128)}, u32[]{:S(2)}) copy-start(f32[512,256]{1,0:T(8,128)} %param.13) | copy-start | bytes 1572868
  6.5 987.7 %reduce-scatter.4.cloned.1.call-start = ((), (), s32[]{:S(2)}) async-start(), calls=%async_computation.1 | async-start | bytes 393216
  6.5 198.1 %collective-permute-start.9 = (bf16[2,2,256,256]{3,2,1,0:T(8,128)(2,1)}, bf16[2,2,256,256]{3,2,1,0:T(8,128)(2,1)}, u32[]{:S(2)}, u32[]{:S(2)}) collective-permute-start(bf16[2,2,256,256]{3,2,1,0:T(8,128)(2,1)} %param.9), channel_id=1, source_target_pairs={{0,2},{2,4},{4,6},{6,8},{8,10},{10,12},{12,14},{14,16},{16,18},{18... | collective-permute-start | bytes 1572872 | tf_op jit(solution)/shard_map/ppermute | solution.py:22
  8.6 197.9 %collective-permute-start.15 = (bf16[2,2,256,256]{3,2,1,0:T(8,128)(2,1)}, bf16[2,2,256,256]{3,2,1,0:T(8,128)(2,1)}, u32[]{:S(2)}, u32[]{:S(2)}) collective-permute-start(bf16[2,2,256,256]{3,2,1,0:T(8,128)(2,1)} %param.9), channel_id=1, source_target_pairs={{0,254},{2,0},{4,2},{6,4},{8,6},{10,8},{12,10},{14,12},{16,14},{18... | collective-permute-start | bytes 1572872 | tf_op jit(solution)/shard_map/ppermute | solution.py:22
  19.4 177.4 %collective-permute-start.10 = (bf16[2,2,64,512]{3,2,1,0:T(8,128)(2,1)}, bf16[2,2,64,512]{3,2,1,0:T(8,128)(2,1)}, u32[]{:S(2)}, u32[]{:S(2)}) collective-permute-start(bf16[2,2,64,512]{3,2,1,0:T(8,128)(2,1)} %param.10), channel_id=1, source_target_pairs={{0,2},{2,4},{4,6},{6,8},{8,10},{10,12},{12,14},{14,16},{16,18},{18... | collective-permute-start | bytes 786440 | tf_op jit(solution)/shard_map/ppermute | solution.py:22
  21.3 177.5 %collective-permute-start.16 = (bf16[2,2,64,512]{3,2,1,0:T(8,128)(2,1)}, bf16[2,2,64,512]{3,2,1,0:T(8,128)(2,1)}, u32[]{:S(2)}, u32[]{:S(2)}) collective-permute-start(bf16[2,2,64,512]{3,2,1,0:T(8,128)(2,1)} %param.10), channel_id=1, source_target_pairs={{0,254},{2,0},{4,2},{6,4},{8,6},{10,8},{12,10},{14,12},{16,14},{18... | collective-permute-start | bytes 786440 | tf_op jit(solution)/shard_map/ppermute | solution.py:22
  28.1 40.2 %collective-permute-start = (bf16[2,2,2,64,256]{4,3,0,2,1:T(8,128)(2,1)S(1)}, bf16[2,2,2,64,256]{4,3,0,2,1:T(8,128)(2,1)S(1)}, u32[]{:S(2)}, u32[]{:S(2)}) collective-permute-start(bf16[2,2,2,64,256]{4,3,0,2,1:T(8,128)(2,1)S(1)} %bitcast.651), channel_id=1, source_target_pairs={{0,256},{256,0},{1,257},{257,1},{2,258},{258,2},{3,259},{259,3},{4... | collective-permute-start | bytes 786440 | tf_op jit(solution)/shard_map/ppermute | solution.py:17
  68.3 4.2 collective-permute-start.1
  72.5 10.7 collective-permute-start.2
  83.2 16.3 %collective-permute-start.3 = (bf16[2,2,2,64,256]{4,3,0,2,1:T(8,128)(2,1)S(1)}, bf16[2,2,2,64,256]{4,3,0,2,1:T(8,128)(2,1)S(1)}, u32[]{:S(2)}, u32[]{:S(2)}) collective-permute-start(bf16[2,2,2,64,256]{4,3,0,2,1:T(8,128)(2,1)S(1)} %collective-permute-done.2), channel_id=1, source_target_pairs={{0,8},{8,0},{2,10},{10,2},{4,12},{12,4},{6,14},{14,6},{16,24},{24,... | collective-permute-start | bytes 786440 | tf_op jit(solution)/shard_map/ppermute | solution.py:17
  99.5 27.1 %collective-permute-start.4 = (bf16[2,2,2,64,256]{4,3,0,2,1:T(8,128)(2,1)S(1)}, bf16[2,2,2,64,256]{4,3,0,2,1:T(8,128)(2,1)S(1)}, u32[]{:S(2)}, u32[]{:S(2)}) collective-permute-start(bf16[2,2,2,64,256]{4,3,0,2,1:T(8,128)(2,1)S(1)} %collective-permute-done.3), channel_id=1, source_target_pairs={{0,16},{16,0},{2,18},{18,2},{4,20},{20,4},{6,22},{22,6},{8,24},{24... | collective-permute-start | bytes 786440 | tf_op jit(solution)/shard_map/ppermute | solution.py:17
  126.6 31.6 %collective-permute-start.5 = (bf16[2,2,2,64,256]{4,3,0,2,1:T(8,128)(2,1)S(1)}, bf16[2,2,2,64,256]{4,3,0,2,1:T(8,128)(2,1)S(1)}, u32[]{:S(2)}, u32[]{:S(2)}) collective-permute-start(bf16[2,2,2,64,256]{4,3,0,2,1:T(8,128)(2,1)S(1)} %collective-permute-done.4), channel_id=1, source_target_pairs={{0,32},{32,0},{2,34},{34,2},{4,36},{36,4},{6,38},{38,6},{8,40},{40... | collective-permute-start | bytes 786440 | tf_op jit(solution)/shard_map/ppermute | solution.py:17
  158.2 10.2 collective-permute-start.6
  168.4 43.9 %collective-permute-start.7 = (bf16[2,2,2,64,256]{4,3,0,2,1:T(8,128)(2,1)}, bf16[2,2,2,64,256]{4,3,0,2,1:T(8,128)(2,1)}, u32[]{:S(2)}, u32[]{:S(2)}) collective-permute-start(bf16[2,2,2,64,256]{4,3,0,2,1:T(8,128)(2,1)} %collective-permute-done.6), channel_id=1, source_target_pairs={{0,128},{128,0},{2,130},{130,2},{4,132},{132,4},{6,134},{134,6},{8... | collective-permute-start | bytes 786440 | tf_op jit(solution)/shard_map/ppermute | solution.py:17
  196.8 658.7 %collective-permute-start.13 = (bf16[2,2,64,512]{3,2,1,0:T(8,128)(2,1)}, bf16[2,2,64,512]{3,2,1,0:T(8,128)(2,1)}, u32[]{:S(2)}, u32[]{:S(2)}) collective-permute-start(bf16[2,2,64,512]{3,2,1,0:T(8,128)(2,1)} %collective-permute-done.10), channel_id=1, source_target_pairs={{0,2},{2,4},{4,6},{6,8},{8,10},{10,12},{12,14},{14,16},{16,18},{18... | collective-permute-start | bytes 786440 | tf_op jit(solution)/shard_map/ppermute | solution.py:22
  198.8 669.1 %collective-permute-start.19 = (bf16[2,2,64,512]{3,2,1,0:T(8,128)(2,1)}, bf16[2,2,64,512]{3,2,1,0:T(8,128)(2,1)}, u32[]{:S(2)}, u32[]{:S(2)}) collective-permute-start(bf16[2,2,64,512]{3,2,1,0:T(8,128)(2,1)} %collective-permute-done.16), channel_id=1, source_target_pairs={{0,254},{2,0},{4,2},{6,4},{8,6},{10,8},{12,10},{14,12},{16,14},{18... | collective-permute-start | bytes 786440 | tf_op jit(solution)/shard_map/ppermute | solution.py:22
  204.6 641.0 %collective-permute-start.12 = (bf16[2,2,256,256]{3,2,1,0:T(8,128)(2,1)}, bf16[2,2,256,256]{3,2,1,0:T(8,128)(2,1)}, u32[]{:S(2)}, u32[]{:S(2)}) collective-permute-start(bf16[2,2,256,256]{3,2,1,0:T(8,128)(2,1)} %collective-permute-done.9), channel_id=1, source_target_pairs={{0,2},{2,4},{4,6},{6,8},{8,10},{10,12},{12,14},{14,16},{16,18},{18... | collective-permute-start | bytes 1572872 | tf_op jit(solution)/shard_map/ppermute | solution.py:22
  206.5 656.7 %collective-permute-start.18 = (bf16[2,2,256,256]{3,2,1,0:T(8,128)(2,1)}, bf16[2,2,256,256]{3,2,1,0:T(8,128)(2,1)}, u32[]{:S(2)}, u32[]{:S(2)}) collective-permute-start(bf16[2,2,256,256]{3,2,1,0:T(8,128)(2,1)} %collective-permute-done.15), channel_id=1, source_target_pairs={{0,254},{2,0},{4,2},{6,4},{8,6},{10,8},{12,10},{14,12},{16,14},{18... | collective-permute-start | bytes 1572872 | tf_op jit(solution)/shard_map/ppermute | solution.py:22
  221.3 594.7 %collective-permute-start.8 = (bf16[2,2,2,64,256]{4,3,0,2,1:T(8,128)(2,1)}, bf16[2,2,2,64,256]{4,3,0,2,1:T(8,128)(2,1)}, u32[]{:S(2)}, u32[]{:S(2)}) collective-permute-start(bf16[2,2,2,64,256]{4,3,0,2,1:T(8,128)(2,1)} %fusion.89), channel_id=1, source_target_pairs={{0,2},{2,4},{4,6},{6,8},{8,10},{10,12},{12,14},{14,16},{16,18},{18... | collective-permute-start | bytes 786440 | tf_op jit(solution)/shard_map/ppermute | solution.py:22
  228.5 584.7 %copy-start.45 = (bf16[2,2,64,256]{3,2,1,0:T(8,128)(2,1)S(1)}, bf16[2,2,64,256]{3,2,1,0:T(8,128)(2,1)}, u32[]{:S(2)}) copy-start(bf16[2,2,64,256]{3,2,1,0:T(8,128)(2,1)} %get-tuple-element.66) | copy-start | bytes 393220
  816.0 14.6 %collective-permute-start.14 = (bf16[2,2,2,64,256]{4,3,0,2,1:T(8,128)(2,1)}, bf16[2,2,2,64,256]{4,3,0,2,1:T(8,128)(2,1)S(1)}, u32[]{:S(2)}, u32[]{:S(2)}) collective-permute-start(bf16[2,2,2,64,256]{4,3,0,2,1:T(8,128)(2,1)} %fusion.89), channel_id=1, source_target_pairs={{0,254},{2,0},{4,2},{6,4},{8,6},{10,8},{12,10},{14,12},{16,14},{18... | collective-permute-start | bytes 786440 | tf_op jit(solution)/shard_map/ppermute | solution.py:22
  830.6 20.3 %collective-permute-start.11 = (bf16[2,2,2,64,256]{4,3,0,2,1:T(8,128)(2,1)}, bf16[2,2,2,64,256]{4,3,0,2,1:T(8,128)(2,1)S(1)}, u32[]{:S(2)}, u32[]{:S(2)}) collective-permute-start(bf16[2,2,2,64,256]{4,3,0,2,1:T(8,128)(2,1)} %collective-permute-done.8), channel_id=1, source_target_pairs={{0,2},{2,4},{4,6},{6,8},{8,10},{10,12},{12,14},{14,16},{16,18},{18... | collective-permute-start | bytes 786440 | tf_op jit(solution)/shard_map/ppermute | solution.py:22
  845.6 17.6 %collective-permute-start.17 = (bf16[2,2,2,64,256]{4,3,0,2,1:T(8,128)(2,1)S(1)}, bf16[2,2,2,64,256]{4,3,0,2,1:T(8,128)(2,1)S(1)}, u32[]{:S(2)}, u32[]{:S(2)}) collective-permute-start(bf16[2,2,2,64,256]{4,3,0,2,1:T(8,128)(2,1)S(1)} %collective-permute-done.14), channel_id=1, source_target_pairs={{0,254},{2,0},{4,2},{6,4},{8,6},{10,8},{12,10},{14,12},{16,14},{18... | collective-permute-start | bytes 786440 | tf_op jit(solution)/shard_map/ppermute | solution.py:22
  900.7 182.2 %copy-start.1 = (f32[512,256]{1,0:T(8,128)S(1)}, f32[512,256]{1,0:T(8,128)}, u32[]{:S(2)}) copy-start(f32[512,256]{1,0:T(8,128)} %param.13) | copy-start | bytes 1572868
  996.5 7.1 collective-permute-start.20
  1003.7 3.2 collective-permute-start.21
  1007.0 7.4 collective-permute-start.22
  1014.4 10.3 collective-permute-start.23
  1024.7 17.5 %collective-permute-start.24 = (bf16[2,2,2,64,128]{4,3,0,2,1:T(8,128)(2,1)S(1)}, bf16[2,2,2,64,128]{4,3,0,2,1:T(8,128)(2,1)S(1)}, u32[]{:S(2)}, u32[]{:S(2)}) collective-permute-start(bf16[2,2,2,64,128]{4,3,0,2,1:T(8,128)(2,1)S(1)} %collective-permute-done.23), channel_id=1, source_target_pairs={{0,16},{16,0},{2,18},{18,2},{4,20},{20,4},{6,22},{22,6},{8,24},{24... | collective-permute-start | bytes 393224 | tf_op jit(solution)/shard_map/ppermute | solution.py:17
  1042.2 24.1 %collective-permute-start.25 = (bf16[2,2,2,64,128]{4,3,0,2,1:T(8,128)(2,1)S(1)}, bf16[2,2,2,64,128]{4,3,0,2,1:T(8,128)(2,1)S(1)}, u32[]{:S(2)}, u32[]{:S(2)}) collective-permute-start(bf16[2,2,2,64,128]{4,3,0,2,1:T(8,128)(2,1)S(1)} %collective-permute-done.24), channel_id=1, source_target_pairs={{0,32},{32,0},{2,34},{34,2},{4,36},{36,4},{6,38},{38,6},{8,40},{40... | collective-permute-start | bytes 393224 | tf_op jit(solution)/shard_map/ppermute | solution.py:17
  1066.3 6.8 collective-permute-start.26
  1073.2 8.4 collective-permute-start.27
  (57 other events, 547.8 us)
Sparse Core Ops, SparseCore 0:
  901.9 92.3 reduce-scatter.3
where the time goes:
time: 1100 us; the launch traced here: 1090 us
  blocking collectives  583 us (53%)
  waiting for transfers between devices  201 us (18%)
  starting transfers between devices  120 us (11%)
  matrix products  76.2 us (7%)
  other arithmetic  56.5 us (5%)
  local copies, waits for them, and re-layouts  38.9 us (4%)
  between operations  15.1 us (1%)
    psum x1, blocking collectives, per_device(): spread = lax.psum(spread, ('ka', 'isdf'))  583 us
    ppermute x16, waiting for transfers between devices, swapped(): return lax.ppermute(block, axis, route)  108 us
    unnamed x2, waiting for transfers between devices  92.5 us
    ppermute x16, starting transfers between devices, swapped(): return lax.ppermute(block, axis, route)  71.8 us
    dot_general x48, matrix products, single(): jnp.einsum(pattern, first, second, preferred_element_type=jnp.float32)  53.3 us
    ppermute x12, starting transfers between devices, shifted(): lax.ppermute(value, axis, [(i, (i + by) % size) for i in range(size)])  47.7 us
    dot_general x10, matrix products, accumulate(): jnp.einsum('kw,wrmn->rkmn', selector[:, visitor], screened, preferred_ele...  22.4 us
  transfers between devices with their start and end apart: 29, of which 14 were waited for; matrix products, arithmetic and copies ran while one was open for 12% of the time, Pallas kernels for 0%

commit v1 on v0

--- a/solution.py
+++ b/solution.py
@@ -96,7 +96,7 @@
     )
     density = jnp.stack([rho_real, rho_imag], axis=1)
     spread = jnp.einsum("nm,brm->brn", coulomb, density, precision=HIGHEST)
-    spread = lax.psum(spread, ("ka", "isdf"))
+    spread = lax.psum(lax.psum(spread, "ka"), "isdf")
     potential = lax.dynamic_slice_in_dim(spread, isdf_index * mu_count, mu_count, 2)
     class_ids = jnp.arange(screened.shape[0], dtype=jnp.int32)
 

time: 1100 us -> 704 us (0.64)
  the two profiles are of different devices: /device:TPU:2 before, /device:TPU:6 now
where the time goes in v1:
time: 704 us; the launch traced here: 694 us
  blocking collectives  223 us (32%)
  waiting for transfers between devices  166 us (24%)
  starting transfers between devices  118 us (17%)
  matrix products  76.2 us (11%)
  other arithmetic  56.4 us (8%)
  local copies, waits for them, and re-layouts  38.9 us (6%)
  between operations  15.1 us (2%)
    psum x2, blocking collectives, per_device(): spread = lax.psum(lax.psum(spread, 'ka'), 'isdf')  223 us
    ppermute x16, waiting for transfers between devices, swapped(): return lax.ppermute(block, axis, route)  109 us
    ppermute x16, starting transfers between devices, swapped(): return lax.ppermute(block, axis, route)  70.1 us
    unnamed x2, waiting for transfers between devices  57.2 us
    dot_general x48, matrix products, single(): jnp.einsum(pattern, first, second, preferred_element_type=jnp.float32)  53.3 us
    ppermute x12, starting transfers between devices, shifted(): lax.ppermute(value, axis, [(i, (i + by) % size) for i in range(size)])  48 us
    dot_general x10, matrix products, accumulate(): jnp.einsum('kw,wrmn->rkmn', selector[:, visitor], screened, preferred_ele...  22.3 us
    mul x10, other arithmetic, accumulate(): screen_real * visit_real - screen_imag * visit_imag  21.6 us
  transfers between devices with their start and end apart: 29, of which 14 were waited for; matrix products, arithmetic and copies ran while one was open for 19% of the time, Pallas kernels for 0%

profile of v1, /device:TPU:6, one launch (start us, length us, event | category | flops | bytes accessed | tf_op | source)
XLA Modules:
  0.0 693.6 jit_solution(5122850828781368609)
XLA Ops:
  8.6 11.1 %collective-permute-start.15 = (bf16[2,2,256,256]{3,2,1,0:T(8,128)(2,1)}, bf16[2,2,256,256]{3,2,1,0:T(8,128)(2,1)}, u32[]{:S(2)}, u32[]{:S(2)}) collective-permute-start(bf16[2,2,256,256]{3,2,1,0:T(8,128)(2,1)} %param.9), channel_id=1, source_target_pairs={{0,254},{2,0},{4,2},{6,4},{8,6},{10,8},{12,10},{14,12},{16,14},{18... | collective-permute-start | bytes 1572872 | tf_op jit(solution)/shard_map/ppermute | solution.py:22
  21.6 5.8 collective-permute-start.16
  28.4 3.5 collective-permute-start
  33.1 3.2 copy.91
  59.3 3.0 fusion.79
  76.9 6.6 collective-permute-done.2
  87.4 12.3 %collective-permute-done.3 = bf16[2,2,2,64,256]{4,3,0,2,1:T(8,128)(2,1)S(1)} collective-permute-done((bf16[2,2,2,64,256]{4,3,0,2,1:T(8,128)(2,1)S(1)}, bf16[2,2,2,64,256]{4,3,0,2,1:T(8,128)(2,1)S(1)}, u32[]{:S(2)}, u32[]{:S(2)}) %collective-permute-start.3) | collective-permute-done | bytes 262176 | tf_op jit(solution)/shard_map/ppermute | solution.py:17
  103.9 23.0 %collective-permute-done.4 = bf16[2,2,2,64,256]{4,3,0,2,1:T(8,128)(2,1)S(1)} collective-permute-done((bf16[2,2,2,64,256]{4,3,0,2,1:T(8,128)(2,1)S(1)}, bf16[2,2,2,64,256]{4,3,0,2,1:T(8,128)(2,1)S(1)}, u32[]{:S(2)}, u32[]{:S(2)}) %collective-permute-start.4) | collective-permute-done | bytes 262176 | tf_op jit(solution)/shard_map/ppermute | solution.py:17
  126.9 14.4 %collective-permute-start.5 = (bf16[2,2,2,64,256]{4,3,0,2,1:T(8,128)(2,1)S(1)}, bf16[2,2,2,64,256]{4,3,0,2,1:T(8,128)(2,1)S(1)}, u32[]{:S(2)}, u32[]{:S(2)}) collective-permute-start(bf16[2,2,2,64,256]{4,3,0,2,1:T(8,128)(2,1)S(1)} %collective-permute-done.4), channel_id=1, source_target_pairs={{0,32},{32,0},{2,34},{34,2},{4,36},{36,4},{6,38},{38,6},{8,40},{40... | collective-permute-start | bytes 786440 | tf_op jit(solution)/shard_map/ppermute | solution.py:17
  143.3 14.9 %collective-permute-done.5 = bf16[2,2,2,64,256]{4,3,0,2,1:T(8,128)(2,1)S(1)} collective-permute-done((bf16[2,2,2,64,256]{4,3,0,2,1:T(8,128)(2,1)S(1)}, bf16[2,2,2,64,256]{4,3,0,2,1:T(8,128)(2,1)S(1)}, u32[]{:S(2)}, u32[]{:S(2)}) %collective-permute-start.5) | collective-permute-done | bytes 262176 | tf_op jit(solution)/shard_map/ppermute | solution.py:17
  163.1 5.3 collective-permute-done.6
  168.4 3.5 collective-permute-start.7
  198.0 5.8 collective-permute-start.19
  205.7 5.8 collective-permute-start.18
  227.7 216.0 %psum.14 = f32[2,2,512]{2,1,0:T(2,128)S(1)} all-reduce(f32[2,2,512]{2,1,0:T(2,128)S(1)} %fusion.90), channel_id=1, replica_groups=mesh['pm'=2,'ka'=128,'isdf'=2] {'ka'}, use_global_device_ids=true, to_apply=%region_0.1 | all-reduce | flops 2048 | bytes 16384 | tf_op jit(solution)/shard_map/psum | solution.py:99
  443.7 6.5 psum.15
  484.3 5.3 collective-permute-start.17
  517.3 9.2 %add_convert_fusion = bf16[2,2,256,512]{3,2,0,1:T(8,128)(2,1)S(1)} fusion(f32[2,256,512]{2,1,0:T(8,128)} %get-tuple-element.48, f32[2,256,512]{2,1,0:T(8,128)S(1)} %copy-done.14, f32[2,256,512]{2,1,0:T(8,128)} %get-tuple-element.69, f32[2,256,512]{2,1,0:T(8,128)S(1)} %copy-done.13, f32[2,256,512]{2,1,0:T(8,128)} %get-tuple-element.47, ...), kind=kLoop, calls=%fused_computation.2 | loop fusion | flops 20971520 | bytes 42991616 | tf_op jit(solution)/shard_map/convert_element_type | solution.py:151
  526.6 9.5 %add_convert_fusion.1 = bf16[2,2,256,512]{3,2,0,1:T(8,128)(2,1)S(1)} fusion(f32[2,256,512]{2,1,0:T(8,128)} %get-tuple-element.48, f32[2,256,512]{2,1,0:T(8,128)S(1)} %copy-done.14, f32[2,256,512]{2,1,0:T(8,128)} %get-tuple-element.69, f32[2,256,512]{2,1,0:T(8,128)S(1)} %copy-done.13, f32[2,256,512]{2,1,0:T(8,128)} %get-tuple-element.47, ...), kind=kLoop, calls=%fused_computation.3 | loop fusion | flops 20971520 | bytes 42991616 | tf_op jit(solution)/shard_map/convert_element_type | solution.py:150
  540.4 57.2 %reduce-scatter.4.cloned.1.call-done = bf16[128,512]{1,0:T(8,128)(2,1)} async-done(((bf16[256,512]{1,0:T(8,128)(2,1)}), bf16[128,512]{1,0:T(8,128)(2,1)}) %reduce-scatter.4.cloned.1.call-update) | async-done | bytes 131088
  602.4 4.6 collective-permute-done.20
  610.3 3.5 collective-permute-start.22
  613.8 4.0 collective-permute-done.22
  617.7 4.5 collective-permute-start.23
  622.2 5.8 collective-permute-done.23
  628.1 7.6 %collective-permute-start.24 = (bf16[2,2,2,64,128]{4,3,0,2,1:T(8,128)(2,1)S(1)}, bf16[2,2,2,64,128]{4,3,0,2,1:T(8,128)(2,1)S(1)}, u32[]{:S(2)}, u32[]{:S(2)}) collective-permute-start(bf16[2,2,2,64,128]{4,3,0,2,1:T(8,128)(2,1)S(1)} %collective-permute-done.23), channel_id=1, source_target_pairs={{0,16},{16,0},{2,18},{18,2},{4,20},{20,4},{6,22},{22,6},{8,24},{24... | collective-permute-start | bytes 393224 | tf_op jit(solution)/shard_map/ppermute | solution.py:17
  635.7 9.9 %collective-permute-done.24 = bf16[2,2,2,64,128]{4,3,0,2,1:T(8,128)(2,1)S(1)} collective-permute-done((bf16[2,2,2,64,128]{4,3,0,2,1:T(8,128)(2,1)S(1)}, bf16[2,2,2,64,128]{4,3,0,2,1:T(8,128)(2,1)S(1)}, u32[]{:S(2)}, u32[]{:S(2)}) %collective-permute-start.24) | collective-permute-done | bytes 131104 | tf_op jit(solution)/shard_map/ppermute | solution.py:17
  645.6 12.0 %collective-permute-start.25 = (bf16[2,2,2,64,128]{4,3,0,2,1:T(8,128)(2,1)S(1)}, bf16[2,2,2,64,128]{4,3,0,2,1:T(8,128)(2,1)S(1)}, u32[]{:S(2)}, u32[]{:S(2)}) collective-permute-start(bf16[2,2,2,64,128]{4,3,0,2,1:T(8,128)(2,1)S(1)} %collective-permute-done.24), channel_id=1, source_target_pairs={{0,32},{32,0},{2,34},{34,2},{4,36},{36,4},{6,38},{38,6},{8,40},{40... | collective-permute-start | bytes 393224 | tf_op jit(solution)/shard_map/ppermute | solution.py:17
  657.6 12.1 %collective-permute-done.25 = bf16[2,2,2,64,128]{4,3,0,2,1:T(8,128)(2,1)S(1)} collective-permute-done((bf16[2,2,2,64,128]{4,3,0,2,1:T(8,128)(2,1)S(1)}, bf16[2,2,2,64,128]{4,3,0,2,1:T(8,128)(2,1)S(1)}, u32[]{:S(2)}, u32[]{:S(2)}) %collective-permute-start.25) | collective-permute-done | bytes 131104 | tf_op jit(solution)/shard_map/ppermute | solution.py:17
  672.3 4.2 collective-permute-done.26
  676.5 3.2 collective-permute-start.27
  679.8 5.1 collective-permute-done.27
  (286 shorter events, 180.2 us)
Async XLA Ops:
  6.5 220.6 %copy-start = (f32[512,256]{1,0:T(8,128)S(1)}, f32[512,256]{1,0:T(8,128)}, u32[]{:S(2)}) copy-start(f32[512,256]{1,0:T(8,128)} %param.13) | copy-start | bytes 1572868
  6.5 591.1 %reduce-scatter.4.cloned.1.call-start = ((), (), s32[]{:S(2)}) async-start(), calls=%async_computation.1 | async-start | bytes 393216
  6.5 197.3 %collective-permute-start.9 = (bf16[2,2,256,256]{3,2,1,0:T(8,128)(2,1)}, bf16[2,2,256,256]{3,2,1,0:T(8,128)(2,1)}, u32[]{:S(2)}, u32[]{:S(2)}) collective-permute-start(bf16[2,2,256,256]{3,2,1,0:T(8,128)(2,1)} %param.9), channel_id=1, source_target_pairs={{0,2},{2,4},{4,6},{6,8},{8,10},{10,12},{12,14},{14,16},{16,18},{18... | collective-permute-start | bytes 1572872 | tf_op jit(solution)/shard_map/ppermute | solution.py:22
  8.6 197.1 %collective-permute-start.15 = (bf16[2,2,256,256]{3,2,1,0:T(8,128)(2,1)}, bf16[2,2,256,256]{3,2,1,0:T(8,128)(2,1)}, u32[]{:S(2)}, u32[]{:S(2)}) collective-permute-start(bf16[2,2,256,256]{3,2,1,0:T(8,128)(2,1)} %param.9), channel_id=1, source_target_pairs={{0,254},{2,0},{4,2},{6,4},{8,6},{10,8},{12,10},{14,12},{16,14},{18... | collective-permute-start | bytes 1572872 | tf_op jit(solution)/shard_map/ppermute | solution.py:22
  19.7 176.3 %collective-permute-start.10 = (bf16[2,2,64,512]{3,2,1,0:T(8,128)(2,1)}, bf16[2,2,64,512]{3,2,1,0:T(8,128)(2,1)}, u32[]{:S(2)}, u32[]{:S(2)}) collective-permute-start(bf16[2,2,64,512]{3,2,1,0:T(8,128)(2,1)} %param.10), channel_id=1, source_target_pairs={{0,2},{2,4},{4,6},{6,8},{8,10},{10,12},{12,14},{14,16},{16,18},{18... | collective-permute-start | bytes 786440 | tf_op jit(solution)/shard_map/ppermute | solution.py:22
  21.6 176.4 %collective-permute-start.16 = (bf16[2,2,64,512]{3,2,1,0:T(8,128)(2,1)}, bf16[2,2,64,512]{3,2,1,0:T(8,128)(2,1)}, u32[]{:S(2)}, u32[]{:S(2)}) collective-permute-start(bf16[2,2,64,512]{3,2,1,0:T(8,128)(2,1)} %param.10), channel_id=1, source_target_pairs={{0,254},{2,0},{4,2},{6,4},{8,6},{10,8},{12,10},{14,12},{16,14},{18... | collective-permute-start | bytes 786440 | tf_op jit(solution)/shard_map/ppermute | solution.py:22
  28.4 40.2 %collective-permute-start = (bf16[2,2,2,64,256]{4,3,0,2,1:T(8,128)(2,1)S(1)}, bf16[2,2,2,64,256]{4,3,0,2,1:T(8,128)(2,1)S(1)}, u32[]{:S(2)}, u32[]{:S(2)}) collective-permute-start(bf16[2,2,2,64,256]{4,3,0,2,1:T(8,128)(2,1)S(1)} %bitcast.651), channel_id=1, source_target_pairs={{0,256},{256,0},{1,257},{257,1},{2,258},{258,2},{3,259},{259,3},{4... | collective-permute-start | bytes 786440 | tf_op jit(solution)/shard_map/ppermute | solution.py:17
  68.6 4.2 collective-permute-start.1
  72.8 10.7 %collective-permute-start.2 = (bf16[2,2,2,64,256]{4,3,0,2,1:T(8,128)(2,1)S(1)}, bf16[2,2,2,64,256]{4,3,0,2,1:T(8,128)(2,1)S(1)}, u32[]{:S(2)}, u32[]{:S(2)}) collective-permute-start(bf16[2,2,2,64,256]{4,3,0,2,1:T(8,128)(2,1)S(1)} %collective-permute-done.1), channel_id=1, source_target_pairs={{0,4},{4,0},{2,6},{6,2},{8,12},{12,8},{10,14},{14,10},{16,20},{20,... | collective-permute-start | bytes 786440 | tf_op jit(solution)/shard_map/ppermute | solution.py:17
  83.5 16.3 %collective-permute-start.3 = (bf16[2,2,2,64,256]{4,3,0,2,1:T(8,128)(2,1)S(1)}, bf16[2,2,2,64,256]{4,3,0,2,1:T(8,128)(2,1)S(1)}, u32[]{:S(2)}, u32[]{:S(2)}) collective-permute-start(bf16[2,2,2,64,256]{4,3,0,2,1:T(8,128)(2,1)S(1)} %collective-permute-done.2), channel_id=1, source_target_pairs={{0,8},{8,0},{2,10},{10,2},{4,12},{12,4},{6,14},{14,6},{16,24},{24,... | collective-permute-start | bytes 786440 | tf_op jit(solution)/shard_map/ppermute | solution.py:17
  99.8 27.1 %collective-permute-start.4 = (bf16[2,2,2,64,256]{4,3,0,2,1:T(8,128)(2,1)S(1)}, bf16[2,2,2,64,256]{4,3,0,2,1:T(8,128)(2,1)S(1)}, u32[]{:S(2)}, u32[]{:S(2)}) collective-permute-start(bf16[2,2,2,64,256]{4,3,0,2,1:T(8,128)(2,1)S(1)} %collective-permute-done.3), channel_id=1, source_target_pairs={{0,16},{16,0},{2,18},{18,2},{4,20},{20,4},{6,22},{22,6},{8,24},{24... | collective-permute-start | bytes 786440 | tf_op jit(solution)/shard_map/ppermute | solution.py:17
  126.9 31.3 %collective-permute-start.5 = (bf16[2,2,2,64,256]{4,3,0,2,1:T(8,128)(2,1)S(1)}, bf16[2,2,2,64,256]{4,3,0,2,1:T(8,128)(2,1)S(1)}, u32[]{:S(2)}, u32[]{:S(2)}) collective-permute-start(bf16[2,2,2,64,256]{4,3,0,2,1:T(8,128)(2,1)S(1)} %collective-permute-done.4), channel_id=1, source_target_pairs={{0,32},{32,0},{2,34},{34,2},{4,36},{36,4},{6,38},{38,6},{8,40},{40... | collective-permute-start | bytes 786440 | tf_op jit(solution)/shard_map/ppermute | solution.py:17
  158.2 10.2 %collective-permute-start.6 = (bf16[2,2,2,64,256]{4,3,0,2,1:T(8,128)(2,1)S(1)}, bf16[2,2,2,64,256]{4,3,0,2,1:T(8,128)(2,1)}, u32[]{:S(2)}, u32[]{:S(2)}) collective-permute-start(bf16[2,2,2,64,256]{4,3,0,2,1:T(8,128)(2,1)S(1)} %collective-permute-done.5), channel_id=1, source_target_pairs={{0,64},{64,0},{2,66},{66,2},{4,68},{68,4},{6,70},{70,6},{8,72},{72... | collective-permute-start | bytes 786440 | tf_op jit(solution)/shard_map/ppermute | solution.py:17
  168.4 43.1 %collective-permute-start.7 = (bf16[2,2,2,64,256]{4,3,0,2,1:T(8,128)(2,1)}, bf16[2,2,2,64,256]{4,3,0,2,1:T(8,128)(2,1)}, u32[]{:S(2)}, u32[]{:S(2)}) collective-permute-start(bf16[2,2,2,64,256]{4,3,0,2,1:T(8,128)(2,1)} %collective-permute-done.6), channel_id=1, source_target_pairs={{0,128},{128,0},{2,130},{130,2},{4,132},{132,4},{6,134},{134,6},{8... | collective-permute-start | bytes 786440 | tf_op jit(solution)/shard_map/ppermute | solution.py:17
  196.0 298.2 %collective-permute-start.13 = (bf16[2,2,64,512]{3,2,1,0:T(8,128)(2,1)}, bf16[2,2,64,512]{3,2,1,0:T(8,128)(2,1)}, u32[]{:S(2)}, u32[]{:S(2)}) collective-permute-start(bf16[2,2,64,512]{3,2,1,0:T(8,128)(2,1)} %collective-permute-done.10), channel_id=1, source_target_pairs={{0,2},{2,4},{4,6},{6,8},{8,10},{10,12},{12,14},{14,16},{16,18},{18... | collective-permute-start | bytes 786440 | tf_op jit(solution)/shard_map/ppermute | solution.py:22
  198.0 308.6 %collective-permute-start.19 = (bf16[2,2,64,512]{3,2,1,0:T(8,128)(2,1)}, bf16[2,2,64,512]{3,2,1,0:T(8,128)(2,1)}, u32[]{:S(2)}, u32[]{:S(2)}) collective-permute-start(bf16[2,2,64,512]{3,2,1,0:T(8,128)(2,1)} %collective-permute-done.16), channel_id=1, source_target_pairs={{0,254},{2,0},{4,2},{6,4},{8,6},{10,8},{12,10},{14,12},{16,14},{18... | collective-permute-start | bytes 786440 | tf_op jit(solution)/shard_map/ppermute | solution.py:22
  203.8 280.5 %collective-permute-start.12 = (bf16[2,2,256,256]{3,2,1,0:T(8,128)(2,1)}, bf16[2,2,256,256]{3,2,1,0:T(8,128)(2,1)}, u32[]{:S(2)}, u32[]{:S(2)}) collective-permute-start(bf16[2,2,256,256]{3,2,1,0:T(8,128)(2,1)} %collective-permute-done.9), channel_id=1, source_target_pairs={{0,2},{2,4},{4,6},{6,8},{8,10},{10,12},{12,14},{14,16},{16,18},{18... | collective-permute-start | bytes 1572872 | tf_op jit(solution)/shard_map/ppermute | solution.py:22
  205.7 296.2 %collective-permute-start.18 = (bf16[2,2,256,256]{3,2,1,0:T(8,128)(2,1)}, bf16[2,2,256,256]{3,2,1,0:T(8,128)(2,1)}, u32[]{:S(2)}, u32[]{:S(2)}) collective-permute-start(bf16[2,2,256,256]{3,2,1,0:T(8,128)(2,1)} %collective-permute-done.15), channel_id=1, source_target_pairs={{0,254},{2,0},{4,2},{6,4},{8,6},{10,8},{12,10},{14,12},{16,14},{18... | collective-permute-start | bytes 1572872 | tf_op jit(solution)/shard_map/ppermute | solution.py:22
  220.5 234.2 %collective-permute-start.8 = (bf16[2,2,2,64,256]{4,3,0,2,1:T(8,128)(2,1)}, bf16[2,2,2,64,256]{4,3,0,2,1:T(8,128)(2,1)}, u32[]{:S(2)}, u32[]{:S(2)}) collective-permute-start(bf16[2,2,2,64,256]{4,3,0,2,1:T(8,128)(2,1)} %fusion.89), channel_id=1, source_target_pairs={{0,2},{2,4},{4,6},{6,8},{8,10},{10,12},{12,14},{14,16},{16,18},{18... | collective-permute-start | bytes 786440 | tf_op jit(solution)/shard_map/ppermute | solution.py:22
  227.7 224.2 %copy-start.45 = (bf16[2,2,64,256]{3,2,1,0:T(8,128)(2,1)S(1)}, bf16[2,2,64,256]{3,2,1,0:T(8,128)(2,1)}, u32[]{:S(2)}) copy-start(bf16[2,2,64,256]{3,2,1,0:T(8,128)(2,1)} %get-tuple-element.66) | copy-start | bytes 393220
  454.7 14.6 %collective-permute-start.14 = (bf16[2,2,2,64,256]{4,3,0,2,1:T(8,128)(2,1)}, bf16[2,2,2,64,256]{4,3,0,2,1:T(8,128)(2,1)S(1)}, u32[]{:S(2)}, u32[]{:S(2)}) collective-permute-start(bf16[2,2,2,64,256]{4,3,0,2,1:T(8,128)(2,1)} %fusion.89), channel_id=1, source_target_pairs={{0,254},{2,0},{4,2},{6,4},{8,6},{10,8},{12,10},{14,12},{16,14},{18... | collective-permute-start | bytes 786440 | tf_op jit(solution)/shard_map/ppermute | solution.py:22
  469.3 20.3 %collective-permute-start.11 = (bf16[2,2,2,64,256]{4,3,0,2,1:T(8,128)(2,1)}, bf16[2,2,2,64,256]{4,3,0,2,1:T(8,128)(2,1)S(1)}, u32[]{:S(2)}, u32[]{:S(2)}) collective-permute-start(bf16[2,2,2,64,256]{4,3,0,2,1:T(8,128)(2,1)} %collective-permute-done.8), channel_id=1, source_target_pairs={{0,2},{2,4},{4,6},{6,8},{8,10},{10,12},{12,14},{14,16},{16,18},{18... | collective-permute-start | bytes 786440 | tf_op jit(solution)/shard_map/ppermute | solution.py:22
  484.3 17.6 %collective-permute-start.17 = (bf16[2,2,2,64,256]{4,3,0,2,1:T(8,128)(2,1)S(1)}, bf16[2,2,2,64,256]{4,3,0,2,1:T(8,128)(2,1)S(1)}, u32[]{:S(2)}, u32[]{:S(2)}) collective-permute-start(bf16[2,2,2,64,256]{4,3,0,2,1:T(8,128)(2,1)S(1)} %collective-permute-done.14), channel_id=1, source_target_pairs={{0,254},{2,0},{4,2},{6,4},{8,6},{10,8},{12,10},{14,12},{16,14},{18... | collective-permute-start | bytes 786440 | tf_op jit(solution)/shard_map/ppermute | solution.py:22
  539.4 146.9 %copy-start.1 = (f32[512,256]{1,0:T(8,128)S(1)}, f32[512,256]{1,0:T(8,128)}, u32[]{:S(2)}) copy-start(f32[512,256]{1,0:T(8,128)} %param.13) | copy-start | bytes 1572868
  599.9 7.1 %collective-permute-start.20 = (bf16[2,2,2,64,128]{4,3,0,2,1:T(8,128)(2,1)S(1)}, bf16[2,2,2,64,128]{4,3,0,2,1:T(8,128)(2,1)S(1)}, u32[]{:S(2)}, u32[]{:S(2)}) collective-permute-start(bf16[2,2,2,64,128]{4,3,0,2,1:T(8,128)(2,1)S(1)} %add_convert_fusion.7), channel_id=1, source_target_pairs={{0,256},{256,0},{1,257},{257,1},{2,258},{258,2},{3,259},{259,3},{4... | collective-permute-start | bytes 393224 | tf_op jit(solution)/shard_map/ppermute | solution.py:17
  607.1 3.2 collective-permute-start.21
  610.3 7.4 %collective-permute-start.22 = (bf16[2,2,2,64,128]{4,3,0,2,1:T(8,128)(2,1)S(1)}, bf16[2,2,2,64,128]{4,3,0,2,1:T(8,128)(2,1)S(1)}, u32[]{:S(2)}, u32[]{:S(2)}) collective-permute-start(bf16[2,2,2,64,128]{4,3,0,2,1:T(8,128)(2,1)S(1)} %collective-permute-done.21), channel_id=1, source_target_pairs={{0,4},{4,0},{2,6},{6,2},{8,12},{12,8},{10,14},{14,10},{16,20},{20,... | collective-permute-start | bytes 393224 | tf_op jit(solution)/shard_map/ppermute | solution.py:17
  617.7 10.3 %collective-permute-start.23 = (bf16[2,2,2,64,128]{4,3,0,2,1:T(8,128)(2,1)S(1)}, bf16[2,2,2,64,128]{4,3,0,2,1:T(8,128)(2,1)S(1)}, u32[]{:S(2)}, u32[]{:S(2)}) collective-permute-start(bf16[2,2,2,64,128]{4,3,0,2,1:T(8,128)(2,1)S(1)} %collective-permute-done.22), channel_id=1, source_target_pairs={{0,8},{8,0},{2,10},{10,2},{4,12},{12,4},{6,14},{14,6},{16,24},{24,... | collective-permute-start | bytes 393224 | tf_op jit(solution)/shard_map/ppermute | solution.py:17
  628.1 17.5 %collective-permute-start.24 = (bf16[2,2,2,64,128]{4,3,0,2,1:T(8,128)(2,1)S(1)}, bf16[2,2,2,64,128]{4,3,0,2,1:T(8,128)(2,1)S(1)}, u32[]{:S(2)}, u32[]{:S(2)}) collective-permute-start(bf16[2,2,2,64,128]{4,3,0,2,1:T(8,128)(2,1)S(1)} %collective-permute-done.23), channel_id=1, source_target_pairs={{0,16},{16,0},{2,18},{18,2},{4,20},{20,4},{6,22},{22,6},{8,24},{24... | collective-permute-start | bytes 393224 | tf_op jit(solution)/shard_map/ppermute | solution.py:17
  645.6 24.1 %collective-permute-start.25 = (bf16[2,2,2,64,128]{4,3,0,2,1:T(8,128)(2,1)S(1)}, bf16[2,2,2,64,128]{4,3,0,2,1:T(8,128)(2,1)S(1)}, u32[]{:S(2)}, u32[]{:S(2)}) collective-permute-start(bf16[2,2,2,64,128]{4,3,0,2,1:T(8,128)(2,1)S(1)} %collective-permute-done.24), channel_id=1, source_target_pairs={{0,32},{32,0},{2,34},{34,2},{4,36},{36,4},{6,38},{38,6},{8,40},{40... | collective-permute-start | bytes 393224 | tf_op jit(solution)/shard_map/ppermute | solution.py:17
  669.7 6.8 collective-permute-start.26
  676.5 8.4 %collective-permute-start.27 = (bf16[2,2,2,64,128]{4,3,0,2,1:T(8,128)(2,1)S(1)}, bf16[2,2,2,64,128]{4,3,0,2,1:T(8,128)(2,1)S(1)}, u32[]{:S(2)}, u32[]{:S(2)}) collective-permute-start(bf16[2,2,2,64,128]{4,3,0,2,1:T(8,128)(2,1)S(1)} %collective-permute-done.26), channel_id=1, source_target_pairs={{0,128},{128,0},{2,130},{130,2},{4,132},{132,4},{6,134},{134,6},{8... | collective-permute-start | bytes 393224 | tf_op jit(solution)/shard_map/ppermute | solution.py:17
  (57 other events, 511.1 us)
Sparse Core Ops, SparseCore 0:
  540.6 57.0 reduce-scatter.3
